TPU v7x, 32 devices: a whole 2x2x4 slice. The times are simulated.
32 devices in a mesh: energy: 8 (over y, x, core), mom: 4 (over z).
Axes of the slice: x: 2, y: 2, z: 4, core: 2. Of those that a mesh axis runs over, the one named last changes fastest.
Arguments:
- green: bfloat16 [4, 8, 4, 2, 256, 256], P('mom', 'energy'), may hold values from -6 to 6
- coupling: bfloat16 [2, 256, 256], replicated, may hold values from -0.375 to 0.375
- phonon: bfloat16 [3, 1024, 256], replicated, may hold values from -4 to 4
- shift: int32 [3, 2], replicated, may hold values from 0 to 1
Outputs:
- sigma: bfloat16 [4, 8, 4, 2, 256, 256], P('mom', 'energy')
All inputs are finite; a program needn't handle non-finite values.
Results may differ from a plain program's by a relative error of at most 0.0049.
Values may be sent and summed in bfloat16 or wider, within the bound.
No kernel may reach another device: no remote copies, remote signals or barrier semaphores. Data moves between devices by JAX's collectives and lax.ppermute only.
A program may use at most 64 MiB of HBM per device.

v0:
```python
import jax
import jax.numpy as jnp
from jax import lax
from jax.experimental import pallas as pl
from jax.experimental.pallas import tpu as pltpu
from jax.sharding import PartitionSpec as P

SMAX = 1
HBM = pl.BlockSpec(memory_space=pltpu.HBM)
VMEM = pl.BlockSpec(memory_space=pltpu.VMEM)
SMEM = pl.BlockSpec(memory_space=pltpu.SMEM)
LIMIT = 32 * 1024 * 1024


def passed_along(x, axis, by):
    length = lax.axis_size(axis)
    pairs = [(i, i + by) for i in range(length) if 0 <= i + by < length]
    return lax.ppermute(x, axis, pairs)


def passed_round(x, even_by, odd_by):
    groups, points = lax.axis_size("energy"), lax.axis_size("mom")
    pairs = []
    for group in range(groups):
        by = even_by if group % 2 == 0 else odd_by
        for point in range(points):
            pairs.append((group * points + point, group * points + (point + by) % points))
    return lax.ppermute(x, ("energy", "mom"), pairs)


def after(x, *results):
    return lax.optimization_barrier((x, *results))[0]


def even_group():
    return lax.rem(lax.axis_index("energy"), 2) == 0


def products(blocks, coupling):
    lefts = [
        jnp.dot(coupling, block, preferred_element_type=jnp.float32).astype(jnp.bfloat16)
        for block in blocks
    ]
    return [jnp.dot(left, coupling, preferred_element_type=jnp.float32) for left in lefts]


def load(place, even, part, back=0):
    first, second, at = place
    if first is second:
        return first[at - back, part]
    return jnp.where(even, first[at - back, part], second[at - back, part])


def terms(energy, offset, shift, coupling, phonon, slots, even):
    modes = coupling.shape[0]
    low, high = slots[energy - SMAX], slots[energy]
    sums = None
    for mode in range(modes):
        step = shift[mode, offset]
        if low[0] is high[0] and low[1] is high[1]:
            blocks = [load(high, even, part, step) for part in range(2)]
        else:
            blocks = [
                jnp.where(step > 0, load(low, even, part), load(high, even, part))
                for part in range(2)
            ]
        found = mode_terms(mode, offset, blocks, coupling, phonon)
        sums = found if sums is None else [x + y for x, y in zip(sums, found)]
    return sums


def mode_terms(mode, offset, blocks, coupling, phonon):
    size = coupling.shape[1]
    first, second = products(blocks, coupling[mode])
    real = phonon[offset, pl.ds(2 * mode * size, size), :].astype(jnp.float32)
    imag = phonon[offset, pl.ds((2 * mode + 1) * size, size), :].astype(jnp.float32)
    return [first * real - second * imag, first * imag + second * real]


def add_low(pair, sources, shift, coupling, phonon, even):
    for offset, place in sources:
        for mode in range(coupling.shape[0]):
            blocks = [load(place, even, part) for part in range(2)]
            found = mode_terms(mode, offset, blocks, coupling, phonon)
            step = shift[mode, offset]
            pair[step, 0] += found[0]
            pair[step, 1] += found[1]


def add_edges(pair, sources, shift, coupling, phonon, even):
    for offset, below, above in sources:
        for mode in range(coupling.shape[0]):
            step = shift[mode, offset]
            blocks = [
                jnp.where(step > 0, load(below, even, part), load(above, even, part))
                for part in range(2)
            ]
            found = mode_terms(mode, offset, blocks, coupling, phonon)
            pair[1 - step, 0] += found[0]
            pair[1 - step, 1] += found[1]


class Operands:
    def __init__(self):
        self.arrays = []

    def add(self, array):
        for n, other in enumerate(self.arrays):
            if other is array:
                return n
        self.arrays.append(array)
        return len(self.arrays) - 1

    def place(self, place):
        return (self.add(place[0]), self.add(place[1]), place[2])

    def slots(self, slots, energies):
        used = {slot for energy in energies for slot in (energy - SMAX, energy)}
        return {slot: self.place(slots[slot]) for slot in slots if slot in used}


def at_refs(refs, place):
    return (refs[place[0]], refs[place[1]], place[2])


def estimate(coupling, energies):
    modes, size, _ = coupling.shape
    flops = 128 * energies * modes * size**3
    return pl.CostEstimate(flops=flops, bytes_accessed=1 << 24, transcendentals=0)


def sums_call(energies, sources, args, like, dtype, raw=None):
    _, parts, size, _ = like.shape
    count = len(energies)
    operands = Operands()
    layout = [(offset, operands.slots(slots, energies)) for offset, slots in sources]
    source = operands.add(like) if raw is not None else None

    def kernel(shift, coupling, phonon, *refs):
        out = refs[-1]
        even = even_group()

        def sums():
            for at, energy in enumerate(energies):
                for n, (offset, slots) in enumerate(layout):
                    slots = {slot: at_refs(refs, place) for slot, place in slots.items()}
                    real, imag = terms(energy, offset, shift, coupling, phonon, slots, even)
                    if n > 0:
                        real, imag = real + out[at, 0], imag + out[at, 1]
                    out[at, 0] = real.astype(out.dtype)
                    out[at, 1] = imag.astype(out.dtype)

        if raw is None:
            sums()
        else:
            first, on_even = raw
            sends_raw = even if on_even else jnp.logical_not(even)

            @pl.when(sends_raw)
            def _():
                out[...] = refs[source][first : first + count]

            @pl.when(jnp.logical_not(sends_raw))
            def _():
                sums()

    return pl.pallas_call(
        kernel,
        out_shape=jax.ShapeDtypeStruct((count, parts, size, size), dtype),
        in_specs=[SMEM] + [VMEM] * (2 + len(operands.arrays)),
        out_specs=VMEM,
        compiler_params=pltpu.CompilerParams(vmem_limit_bytes=LIMIT),
        cost_estimate=estimate(args[1], count * len(sources)),
    )(*args, *operands.arrays)


def early_call(energies, offset, args, like):
    shift, coupling, phonon = args
    _, parts, size, _ = like.shape
    count, first = len(energies), energies[0] - SMAX

    def kernel(shift_hbm, coupling_hbm, phonon_hbm, own_hbm, out, *scratch):
        shift, coupling, phonon, own, sems = scratch
        pairs = [(own_hbm.at[pl.ds(first, count + SMAX)], own), (shift_hbm, shift)]
        pairs += [(coupling_hbm, coupling), (phonon_hbm.at[offset], phonon.at[offset])]
        copies = [pltpu.make_async_copy(*pair, sems.at[n]) for n, pair in enumerate(pairs)]
        even = even_group()
        copies[0].start()

        @pl.when(even)
        def _():
            copies[0].wait()
            out[...] = own[:count]

        @pl.when(jnp.logical_not(even))
        def _():
            for copy in copies[1:]:
                copy.start()
            for copy in copies:
                copy.wait()
            slots = {first + n: (own, own, n) for n in range(count + SMAX)}
            for at, energy in enumerate(energies):
                real, imag = terms(energy, offset, shift, coupling, phonon, slots, even)
                out[at, 0] = real.astype(out.dtype)
                out[at, 1] = imag.astype(out.dtype)

    return pl.pallas_call(
        kernel,
        out_shape=jax.ShapeDtypeStruct((count, parts, size, size), like.dtype),
        in_specs=[HBM] * 4,
        out_specs=VMEM,
        scratch_shapes=[
            pltpu.SMEM(shift.shape, shift.dtype),
            pltpu.VMEM(coupling.shape, coupling.dtype),
            pltpu.VMEM(phonon.shape, phonon.dtype),
            pltpu.VMEM((count + SMAX, parts, size, size), like.dtype),
            pltpu.SemaphoreType.DMA((4,)),
        ],
        compiler_params=pltpu.CompilerParams(vmem_limit_bytes=60 * 1024 * 1024),
        cost_estimate=estimate(coupling, count),
    )(shift, coupling, phonon, like)


def pair_call(pair, sources, args, add):
    operands = Operands()
    layout = [(offset, *[operands.place(place) for place in places]) for offset, *places in sources]

    def kernel(shift, coupling, phonon, pair_ref, *refs):
        out = refs[-1]
        out[...] = pair_ref[...]
        found = [(offset, *[at_refs(refs, p) for p in places]) for offset, *places in layout]
        add(out, found, shift, coupling, phonon, even_group())

    return pl.pallas_call(
        kernel,
        out_shape=jax.ShapeDtypeStruct(pair.shape, pair.dtype),
        in_specs=[SMEM] + [VMEM] * (len(args) + len(operands.arrays)),
        out_specs=VMEM,
        compiler_params=pltpu.CompilerParams(vmem_limit_bytes=LIMIT),
        cost_estimate=estimate(args[1], 1),
    )(*args, pair, *operands.arrays)


def add_call(energy, pair, pieces, out):
    _, parts, size, _ = out.shape
    arrays = [place[0] for place in pieces]

    def kernel(pair_ref, *refs):
        result = pair_ref[energy]
        for (_, _, at), ref in zip(pieces, refs):
            result = result + ref[at].astype(jnp.float32)
        refs[-1][0] = result.astype(out.dtype)

    return pl.pallas_call(
        kernel,
        grid=(1,),
        out_shape=jax.ShapeDtypeStruct(out.shape, out.dtype),
        in_specs=[VMEM] * (1 + len(arrays)) + [pl.BlockSpec(memory_space=pl.ANY)],
        out_specs=pl.BlockSpec((1, parts, size, size), lambda i: (i + energy, 0, 0, 0)),
        input_output_aliases={1 + len(arrays): 0},
        compiler_params=pltpu.CompilerParams(vmem_limit_bytes=LIMIT),
        cost_estimate=pl.CostEstimate(flops=1 << 33, bytes_accessed=1 << 24, transcendentals=0),
    )(pair, *arrays, out)


def finish_call(energies, whole, total, sources, pieces, args, out=None):
    _, parts, size, _ = whole
    operands = Operands()
    base = operands.add(total)
    layout = [(offset, operands.slots(slots, energies)) for offset, slots in sources]
    added = {energy: [operands.place(p) for p in pieces[energy]] for energy in energies}

    def kernel(*refs):
        shift, coupling, phonon = refs[: len(args)] if args else (None,) * 3
        refs = refs[len(args) :]
        even = even_group()
        for at, energy in enumerate(energies):

            @pl.when(pl.program_id(0) == at)
            def _():
                results = [refs[base][at, part] for part in range(2)]
                for offset, slots in layout:
                    slots = {slot: at_refs(refs, place) for slot, place in slots.items()}
                    found = terms(energy, offset, shift, coupling, phonon, slots, even)
                    results = [result + term for result, term in zip(results, found)]
                for part in range(2):
                    for place in added[energy]:
                        piece = load(at_refs(refs, place), even, part)
                        results[part] = results[part] + piece.astype(jnp.float32)
                    refs[-1][0, part] = results[part].astype(jnp.bfloat16)

    arrays = [*args, *operands.arrays]
    specs = [SMEM] * min(len(args), 1) + [VMEM] * (len(arrays) - min(len(args), 1))
    aliases = {}
    if out is not None:
        aliases = {len(arrays): 0}
        arrays.append(out)
        specs.append(pl.BlockSpec(memory_space=pl.ANY))
    first = energies[0]
    return pl.pallas_call(
        kernel,
        grid=(len(energies),),
        out_shape=jax.ShapeDtypeStruct(whole, jnp.bfloat16),
        in_specs=specs,
        out_specs=pl.BlockSpec((1, parts, size, size), lambda i: (i + first, 0, 0, 0)),
        input_output_aliases=aliases,
        compiler_params=pltpu.CompilerParams(vmem_limit_bytes=LIMIT),
        cost_estimate=pl.CostEstimate(flops=1 << 33, bytes_accessed=1 << 24, transcendentals=0),
    )(*arrays)


def body(green, coupling, phonon, shift):
    own = green[0, 0]
    whole = own.shape
    last = whole[0] - 1
    offsets = phonon.shape[0]
    radius = (offsets - 1) // 2
    ups = range(1, radius + 1)
    args = (shift.T, coupling, phonon)
    high = tuple(range(2, last + 1))

    def own_slots(block, below=None):
        slots = {energy: (block, block, energy) for energy in range(last + 1)}
        if below is not None:
            slots[-1] = (below, below, 0)
        return slots

    def send(energies, raw, *results, below=None, early=False):
        block = after(own, *results)
        made, arrived = {}, {}
        for q in ups:
            sources = [(radius - q, own_slots(block, below))]
            if early:
                made[q] = early_call(energies, radius - q, args, block)
            else:
                made[q] = sums_call(energies, sources, args, block, jnp.bfloat16, raw)
            ways = (-q, -q) if raw is None else (q, -q) if raw[1] else (-q, q)
            arrived[q] = passed_round(made[q], *ways)
        return list(made.values()), arrived

    own_top = own[last:]
    tops = {q: passed_round(own_top, q, q) for q in ups}
    made, high_1 = send(high, (1, True), own_top, early=True)
    below = passed_along(after(own_top, *made), "energy", 1)
    made, high_2 = send(high, (1, False), *made)
    block = after(own, *made)
    own_high = sums_call(high, [(radius, own_slots(block))], args, own, jnp.float32)
    pair = sums_call((0, 1), [(radius, own_slots(block, below))], args, own, jnp.float32)
    low = after(own, *made, *tops.values())[:1]
    lows = {q: passed_round(low, q, q) for q in ups}
    belows = {q: passed_along(after(tops[q], low), "energy", 1) for q in ups}
    made, second = send((1,), None, *made, low, *high_1.values())
    made, first = send((0,), None, *made, *high_2.values(), below=below)

    sources = []
    pieces = {energy: [] for energy in range(last + 1)}
    for q in ups:
        slots = {slot: (high_1[q], high_2[q], slot - 1) for slot in range(1, last)}
        slots[last] = (tops[q], tops[q], 0)
        slots[-1] = (belows[q], belows[q], 0)
        sources.append((radius + q, slots))
        for energy in high:
            pieces[energy].append((high_2[q], high_1[q], energy - 2))
        pieces[1].append((second[q], second[q], 0))
        pieces[0].append((first[q], first[q], 0))
    out = finish_call(high, whole, own_high, sources, pieces, args)
    edges = [(offset, slots[-1], slots[1]) for offset, slots in sources]
    pair = pair_call(pair, edges, args, add_edges)
    lowest = [(offset, (lows[q], lows[q], 0)) for q, (offset, _) in zip(ups, sources)]
    pair = pair_call(pair, lowest, args, add_low)
    for energy in (1, 0):
        out = add_call(energy, pair, pieces[energy], out)
    return out[None, None]


def solution(mesh):
    placed = (P("mom", "energy", None, None, None, None), P(), P(), P())
    return jax.shard_map(
        body,
        mesh=mesh,
        in_specs=placed,
        out_specs=P("mom", "energy", None, None, None, None),
        check_vma=False,
    )
```

profile of v0, /device:TPU:0, one launch (start us, length us, event | category | flops | bytes accessed | tf_op | source)
XLA Modules:
  0.0 52.5 jit_solution(7812201627411414177)
XLA Ops:
  0.0 1.0 %slice_bitcast_fusion = bf16[1,2,256,256]{3,2,1,0:T(8,128)(2,1)S(1)} fusion(bf16[1,1,4,2,256,256]{5,4,3,2,1,0:T(8,128)(2,1)} %param.4), kind=kLoop, calls=%fused_computation | loop fusion | bytes 524288 | tf_op jit(solution)/shard_map/slice | solution.py:341
  1.0 3.1 %collective-permute-start.1 = (bf16[1,2,256,256]{3,2,1,0:T(8,128)(2,1)S(1)}, bf16[1,2,256,256]{3,2,1,0:T(8,128)(2,1)S(1)}, u32[]{:S(2)}, u32[]{:S(2)}) collective-permute-start(bf16[1,2,256,256]{3,2,1,0:T(8,128)(2,1)S(1)} %slice_bitcast_fusion), channel_id=1, source_target_pairs={{0,1},{1,2},{2,3},{3,0},{4,5},{5,6},{6,7},{7,4},{8,9},{9,10},{10,1... | collective-permute-start | bytes 786440 | tf_op jit(solution)/shard_map/ppermute | solution.py:28
  4.1 2.1 %shard_map.46 = bf16[2,2,256,256]{3,2,1,0:T(8,128)(2,1)} custom-call(s32[2,3]{1,0:T(2,128)} %bitcast.12, bf16[2,256,256]{2,1,0:T(8,128)(2,1)} %refs_1_.1, bf16[3,1024,256]{2,1,0:T(8,128)(2,1)} %refs_2_.1, bf16[4,2,256,256]{3,2,1,0:T(8,128)(2,1)} %bitcast.5), custom_call_target="tpu_custom_call" | custom-call | flops 8589934592 | bytes 16777216 | tf_op jit(solution)/shard_map/pallas_call | solution.py:207
  6.2 1.6 %collective-permute-start.3 = (bf16[2,2,256,256]{3,2,1,0:T(8,128)(2,1)}, bf16[2,2,256,256]{3,2,1,0:T(8,128)(2,1)S(1)}, u32[]{:S(2)}, u32[]{:S(2)}) collective-permute-start(bf16[2,2,256,256]{3,2,1,0:T(8,128)(2,1)} %shard_map.46), channel_id=1, source_target_pairs={{0,1},{1,2},{2,3},{3,0},{4,7},{5,4},{6,5},{7,6},{8,9},{9,10},{10,1... | collective-permute-start | bytes 1572872 | tf_op jit(solution)/shard_map/ppermute | solution.py:28
  7.8 3.2 %collective-permute-start = (bf16[1,2,256,256]{3,2,1,0:T(8,128)(2,1)S(1)}, bf16[1,2,256,256]{3,2,1,0:T(8,128)(2,1)S(1)}, u32[]{:S(2)}, u32[]{:S(2)}) collective-permute-start(bf16[1,2,256,256]{3,2,1,0:T(8,128)(2,1)S(1)} %slice_bitcast_fusion), channel_id=1, source_target_pairs={{0,4},{4,8},{8,12},{12,16},{16,20},{20,24},{24,28},{1,5},{5,9},{9,... | collective-permute-start | bytes 786440 | tf_op jit(solution)/shard_map/ppermute | solution.py:18
  11.1 1.6 %shard_map.47 = bf16[2,2,256,256]{3,2,1,0:T(8,128)(2,1)S(1)} custom-call(s32[2,3]{1,0:T(2,128)S(1)} %bitcast.13, bf16[2,256,256]{2,1,0:T(8,128)(2,1)S(1)} %copy-done.2, bf16[3,1024,256]{2,1,0:T(8,128)(2,1)S(1)} %copy-done.1, bf16[4,2,256,256]{3,2,1,0:T(8,128)(2,1)S(1)} %bitcast.6), custom_call_target="tpu_custom_call" | custom-call | flops 8589934592 | bytes 16777216 | tf_op jit(solution)/shard_map/pallas_call | solution.py:167
  12.7 1.7 %collective-permute-start.4 = (bf16[2,2,256,256]{3,2,1,0:T(8,128)(2,1)S(1)}, bf16[2,2,256,256]{3,2,1,0:T(8,128)(2,1)S(1)}, u32[]{:S(2)}, u32[]{:S(2)}) collective-permute-start(bf16[2,2,256,256]{3,2,1,0:T(8,128)(2,1)S(1)} %shard_map.47), channel_id=1, source_target_pairs={{0,3},{1,0},{2,1},{3,2},{4,5},{5,6},{6,7},{7,4},{8,11},{9,8},{10,9... | collective-permute-start | bytes 1572872 | tf_op jit(solution)/shard_map/ppermute | solution.py:28
  14.5 1.6 %shard_map.53.refs_3_ = f32[2,2,256,256]{3,2,1,0:T(8,128)S(1)} custom-call(s32[2,3]{1,0:T(2,128)S(1)} %bitcast.14, bf16[2,256,256]{2,1,0:T(8,128)(2,1)S(1)} %copy-done.2, bf16[3,1024,256]{2,1,0:T(8,128)(2,1)S(1)} %copy-done.1, bf16[4,2,256,256]{3,2,1,0:T(8,128)(2,1)S(1)} %bitcast.7), custom_call_target="tpu_custom_call" | custom-call | flops 8589934592 | bytes 16777216 | tf_op jit(solution)/shard_map/pallas_call | solution.py:167
  16.1 0.0 collective-permute-done.1.refs_6_
  16.1 0.4 collective-permute-start.5
  16.5 1.3 %collective-permute-start.2 = (bf16[1,2,256,256]{3,2,1,0:T(8,128)(2,1)S(1)}, bf16[1,2,256,256]{3,2,1,0:T(8,128)(2,1)S(1)}, u32[]{:S(2)}, u32[]{:S(2)}) collective-permute-start(bf16[1,2,256,256]{3,2,1,0:T(8,128)(2,1)S(1)} %collective-permute-done.1.refs_6_), channel_id=1, source_target_pairs={{0,4},{4,8},{8,12},{12,16},{16,20},{20,24},{24,28},{1,5},{5,9},{9,... | collective-permute-start | bytes 786440 | tf_op jit(solution)/shard_map/ppermute | solution.py:18
  17.8 1.6 %shard_map.48.pair_ref = f32[2,2,256,256]{3,2,1,0:T(8,128)S(1)} custom-call(s32[2,3]{1,0:T(2,128)S(1)} %bitcast.15, bf16[2,256,256]{2,1,0:T(8,128)(2,1)S(1)} %copy-done.2, bf16[3,1024,256]{2,1,0:T(8,128)(2,1)S(1)} %copy-done.1, bf16[4,2,256,256]{3,2,1,0:T(8,128)(2,1)S(1)} %bitcast.9, bf16[1,2,256,256]{3,2,1,0:T(8,128)(2,1)S(1)} %collective-permute-done.refs_1_), custom_call_target="tpu_custom_call" | custom-call | flops 8589934592 | bytes 16777216 | tf_op jit(solution)/shard_map/pallas_call | solution.py:167
  19.5 4.7 %collective-permute-done.3.refs_1_.refs_4_ = bf16[2,2,256,256]{3,2,1,0:T(8,128)(2,1)S(1)} collective-permute-done((bf16[2,2,256,256]{3,2,1,0:T(8,128)(2,1)}, bf16[2,2,256,256]{3,2,1,0:T(8,128)(2,1)S(1)}, u32[]{:S(2)}, u32[]{:S(2)}) %collective-permute-start.3) | collective-permute-done | bytes 524320 | tf_op jit(solution)/shard_map/ppermute | solution.py:28
  24.1 1.2 %shard_map.51 = bf16[1,2,256,256]{3,2,1,0:T(8,128)(2,1)S(1)} custom-call(s32[2,3]{1,0:T(2,128)S(1)} %bitcast.16, bf16[2,256,256]{2,1,0:T(8,128)(2,1)S(1)} %copy-done.2, bf16[3,1024,256]{2,1,0:T(8,128)(2,1)S(1)} %copy-done.1, bf16[4,2,256,256]{3,2,1,0:T(8,128)(2,1)S(1)} %bitcast.10), custom_call_target="tpu_custom_call" | custom-call | flops 4294967296 | bytes 16777216 | tf_op jit(solution)/shard_map/pallas_call | solution.py:167
  25.3 10.0 %collective-permute-start.7 = (bf16[1,2,256,256]{3,2,1,0:T(8,128)(2,1)S(1)}, bf16[1,2,256,256]{3,2,1,0:T(8,128)(2,1)S(1)}, u32[]{:S(2)}, u32[]{:S(2)}) collective-permute-start(bf16[1,2,256,256]{3,2,1,0:T(8,128)(2,1)S(1)} %shard_map.51), channel_id=1, source_target_pairs={{0,3},{1,0},{2,1},{3,2},{4,7},{5,4},{6,5},{7,6},{8,11},{9,8},{10,9... | collective-permute-start | bytes 786440 | tf_op jit(solution)/shard_map/ppermute | solution.py:28
  35.3 5.2 %collective-permute-done.4.refs_2_.refs_5_ = bf16[2,2,256,256]{3,2,1,0:T(8,128)(2,1)S(1)} collective-permute-done((bf16[2,2,256,256]{3,2,1,0:T(8,128)(2,1)S(1)}, bf16[2,2,256,256]{3,2,1,0:T(8,128)(2,1)S(1)}, u32[]{:S(2)}, u32[]{:S(2)}) %collective-permute-start.4) | collective-permute-done | bytes 524320 | tf_op jit(solution)/shard_map/ppermute | solution.py:28
  40.5 1.2 %shard_map.52 = bf16[1,2,256,256]{3,2,1,0:T(8,128)(2,1)S(1)} custom-call(s32[2,3]{1,0:T(2,128)S(1)} %bitcast.17, bf16[2,256,256]{2,1,0:T(8,128)(2,1)S(1)} %copy-done.2, bf16[3,1024,256]{2,1,0:T(8,128)(2,1)S(1)} %copy-done.1, bf16[4,2,256,256]{3,2,1,0:T(8,128)(2,1)S(1)} %bitcast.11, bf16[1,2,256,256]{3,2,1,0:T(8,128)(2,1)S(1)} %collective-permute-done.refs_1_), custom_call_target="tpu_custom_call" | custom-call | flops 4294967296 | bytes 16777216 | tf_op jit(solution)/shard_map/pallas_call | solution.py:167
  41.7 0.1 collective-permute-start.6
  41.8 2.7 %shard_map.54.refs_1_ = bf16[4,2,256,256]{3,2,1,0:T(8,128)(2,1)} custom-call(s32[2,3]{1,0:T(2,128)S(1)} %bitcast.18, bf16[2,256,256]{2,1,0:T(8,128)(2,1)S(1)} %copy-done.2, bf16[3,1024,256]{2,1,0:T(8,128)(2,1)S(1)} %copy-done.1, f32[2,2,256,256]{3,2,1,0:T(8,128)S(1)} %shard_map.53.refs_3_, ...), custom_call_target="tpu_custom_call" | custom-call | flops 8589934592 | bytes 16777216 | tf_op jit(solution)/shard_map/pallas_call | solution.py:300
  44.5 1.2 %shard_map.49.pair_ref = f32[2,2,256,256]{3,2,1,0:T(8,128)S(1)} custom-call(s32[2,3]{1,0:T(2,128)S(1)} %bitcast.19, bf16[2,256,256]{2,1,0:T(8,128)(2,1)S(1)} %copy-done.2, bf16[3,1024,256]{2,1,0:T(8,128)(2,1)S(1)} %copy-done.1, f32[2,2,256,256]{3,2,1,0:T(8,128)S(1)} %shard_map.48.pair_ref, bf16[1,2,256,256]{3,2,1,0:T(8,128)(2,1)S(1)} %collective-permute-done.2.refs_0_, ...), custom_call_target="tpu_custom_call" | custom-call | flops 4294967296 | bytes 16777216 | tf_op jit(solution)/shard_map/pallas_call | solution.py:234
  45.7 1.2 %shard_map.50.pair_ref = f32[2,2,256,256]{3,2,1,0:T(8,128)S(1)} custom-call(s32[2,3]{1,0:T(2,128)S(1)} %bitcast.20, bf16[2,256,256]{2,1,0:T(8,128)(2,1)S(1)} %copy-done.2, bf16[3,1024,256]{2,1,0:T(8,128)(2,1)S(1)} %copy-done.1, f32[2,2,256,256]{3,2,1,0:T(8,128)S(1)} %shard_map.49.pair_ref, bf16[1,2,256,256]{3,2,1,0:T(8,128)(2,1)S(1)} %collective-permute-done.5.refs_0_), custom_call_target="tpu_custom_call" | custom-call | flops 4294967296 | bytes 16777216 | tf_op jit(solution)/shard_map/pallas_call | solution.py:234
  46.9 0.8 %shard_map.55.refs_1_ = bf16[4,2,256,256]{3,2,1,0:T(8,128)(2,1)} custom-call(f32[2,2,256,256]{3,2,1,0:T(8,128)S(1)} %shard_map.50.pair_ref, bf16[1,2,256,256]{3,2,1,0:T(8,128)(2,1)S(1)} %collective-permute-done.7.refs_0_, bf16[4,2,256,256]{3,2,1,0:T(8,128)(2,1)} %shard_map.54.refs_1_), custom_call_target="tpu_custom_call", output_to_operand_aliasing={{}: (2, {})} | custom-call | flops 8589934592 | bytes 16777216 | tf_op jit(solution)/shard_map/pallas_call | solution.py:254
  47.7 4.1 %collective-permute-done.6.refs_0_ = bf16[1,2,256,256]{3,2,1,0:T(8,128)(2,1)S(1)} collective-permute-done((bf16[1,2,256,256]{3,2,1,0:T(8,128)(2,1)S(1)}, bf16[1,2,256,256]{3,2,1,0:T(8,128)(2,1)S(1)}, u32[]{:S(2)}, u32[]{:S(2)}) %collective-permute-start.6) | collective-permute-done | bytes 262176 | tf_op jit(solution)/shard_map/ppermute | solution.py:28
  51.7 0.7 %shard_map.56 = bf16[4,2,256,256]{3,2,1,0:T(8,128)(2,1)} custom-call(f32[2,2,256,256]{3,2,1,0:T(8,128)S(1)} %shard_map.50.pair_ref, bf16[1,2,256,256]{3,2,1,0:T(8,128)(2,1)S(1)} %collective-permute-done.6.refs_0_, bf16[4,2,256,256]{3,2,1,0:T(8,128)(2,1)} %shard_map.55.refs_1_), custom_call_target="tpu_custom_call", output_to_operand_aliasing={{}: (2, {})} | custom-call | flops 8589934592 | bytes 16777216 | tf_op jit(solution)/shard_map/pallas_call | solution.py:254
  (13 shorter events, 0.0 us)
Async XLA Ops:
  1.0 15.1 %collective-permute-start.1 = (bf16[1,2,256,256]{3,2,1,0:T(8,128)(2,1)S(1)}, bf16[1,2,256,256]{3,2,1,0:T(8,128)(2,1)S(1)}, u32[]{:S(2)}, u32[]{:S(2)}) collective-permute-start(bf16[1,2,256,256]{3,2,1,0:T(8,128)(2,1)S(1)} %slice_bitcast_fusion), channel_id=1, source_target_pairs={{0,1},{1,2},{2,3},{3,0},{4,5},{5,6},{6,7},{7,4},{8,9},{9,10},{10,1... | collective-permute-start | bytes 786440 | tf_op jit(solution)/shard_map/ppermute | solution.py:28
  4.0 7.0 %copy-start = (bf16[1,1,4,2,256,256]{5,4,3,2,1,0:T(8,128)(2,1)S(1)}, bf16[1,1,4,2,256,256]{5,4,3,2,1,0:T(8,128)(2,1)}, u32[]{:S(2)}) copy-start(bf16[1,1,4,2,256,256]{5,4,3,2,1,0:T(8,128)(2,1)} %param.4) | copy-start | bytes 3145732
  4.0 7.0 %copy-start.1 = (bf16[3,1024,256]{2,1,0:T(8,128)(2,1)S(1)}, bf16[3,1024,256]{2,1,0:T(8,128)(2,1)}, u32[]{:S(2)}) copy-start(bf16[3,1024,256]{2,1,0:T(8,128)(2,1)} %refs_2_.1) | copy-start | bytes 4718596
  4.1 7.0 %copy-start.2 = (bf16[2,256,256]{2,1,0:T(8,128)(2,1)S(1)}, bf16[2,256,256]{2,1,0:T(8,128)(2,1)}, u32[]{:S(2)}) copy-start(bf16[2,256,256]{2,1,0:T(8,128)(2,1)} %refs_1_.1) | copy-start | bytes 786436
  4.1 7.0 %copy-start.3 = (s32[3,2]{0,1:T(2,128)S(1)}, s32[3,2]{0,1:T(2,128)}, u32[]{:S(2)}) copy-start(s32[3,2]{0,1:T(2,128)} %param.7) | copy-start | bytes 76
  6.2 17.9 %collective-permute-start.3 = (bf16[2,2,256,256]{3,2,1,0:T(8,128)(2,1)}, bf16[2,2,256,256]{3,2,1,0:T(8,128)(2,1)S(1)}, u32[]{:S(2)}, u32[]{:S(2)}) collective-permute-start(bf16[2,2,256,256]{3,2,1,0:T(8,128)(2,1)} %shard_map.46), channel_id=1, source_target_pairs={{0,1},{1,2},{2,3},{3,0},{4,7},{5,4},{6,5},{7,6},{8,9},{9,10},{10,1... | collective-permute-start | bytes 1572872 | tf_op jit(solution)/shard_map/ppermute | solution.py:28
  7.8 10.0 %collective-permute-start = (bf16[1,2,256,256]{3,2,1,0:T(8,128)(2,1)S(1)}, bf16[1,2,256,256]{3,2,1,0:T(8,128)(2,1)S(1)}, u32[]{:S(2)}, u32[]{:S(2)}) collective-permute-start(bf16[1,2,256,256]{3,2,1,0:T(8,128)(2,1)S(1)} %slice_bitcast_fusion), channel_id=1, source_target_pairs={{0,4},{4,8},{8,12},{12,16},{16,20},{20,24},{24,28},{1,5},{5,9},{9,... | collective-permute-start | bytes 786440 | tf_op jit(solution)/shard_map/ppermute | solution.py:18
  12.7 27.8 %collective-permute-start.4 = (bf16[2,2,256,256]{3,2,1,0:T(8,128)(2,1)S(1)}, bf16[2,2,256,256]{3,2,1,0:T(8,128)(2,1)S(1)}, u32[]{:S(2)}, u32[]{:S(2)}) collective-permute-start(bf16[2,2,256,256]{3,2,1,0:T(8,128)(2,1)S(1)} %shard_map.47), channel_id=1, source_target_pairs={{0,3},{1,0},{2,1},{3,2},{4,5},{5,6},{6,7},{7,4},{8,11},{9,8},{10,9... | collective-permute-start | bytes 1572872 | tf_op jit(solution)/shard_map/ppermute | solution.py:28
  16.1 29.6 %collective-permute-start.5 = (bf16[1,2,256,256]{3,2,1,0:T(8,128)(2,1)S(1)}, bf16[1,2,256,256]{3,2,1,0:T(8,128)(2,1)S(1)}, u32[]{:S(2)}, u32[]{:S(2)}) collective-permute-start(bf16[1,2,256,256]{3,2,1,0:T(8,128)(2,1)S(1)} %slice.11), channel_id=1, source_target_pairs={{0,1},{1,2},{2,3},{3,0},{4,5},{5,6},{6,7},{7,4},{8,9},{9,10},{10,1... | collective-permute-start | bytes 786440 | tf_op jit(solution)/shard_map/ppermute | solution.py:28
  16.5 28.0 %collective-permute-start.2 = (bf16[1,2,256,256]{3,2,1,0:T(8,128)(2,1)S(1)}, bf16[1,2,256,256]{3,2,1,0:T(8,128)(2,1)S(1)}, u32[]{:S(2)}, u32[]{:S(2)}) collective-permute-start(bf16[1,2,256,256]{3,2,1,0:T(8,128)(2,1)S(1)} %collective-permute-done.1.refs_6_), channel_id=1, source_target_pairs={{0,4},{4,8},{8,12},{12,16},{16,20},{20,24},{24,28},{1,5},{5,9},{9,... | collective-permute-start | bytes 786440 | tf_op jit(solution)/shard_map/ppermute | solution.py:18
  25.3 21.6 %collective-permute-start.7 = (bf16[1,2,256,256]{3,2,1,0:T(8,128)(2,1)S(1)}, bf16[1,2,256,256]{3,2,1,0:T(8,128)(2,1)S(1)}, u32[]{:S(2)}, u32[]{:S(2)}) collective-permute-start(bf16[1,2,256,256]{3,2,1,0:T(8,128)(2,1)S(1)} %shard_map.51), channel_id=1, source_target_pairs={{0,3},{1,0},{2,1},{3,2},{4,7},{5,4},{6,5},{7,6},{8,11},{9,8},{10,9... | collective-permute-start | bytes 786440 | tf_op jit(solution)/shard_map/ppermute | solution.py:28
  41.7 10.0 %collective-permute-start.6 = (bf16[1,2,256,256]{3,2,1,0:T(8,128)(2,1)S(1)}, bf16[1,2,256,256]{3,2,1,0:T(8,128)(2,1)S(1)}, u32[]{:S(2)}, u32[]{:S(2)}) collective-permute-start(bf16[1,2,256,256]{3,2,1,0:T(8,128)(2,1)S(1)} %shard_map.52), channel_id=1, source_target_pairs={{0,3},{1,0},{2,1},{3,2},{4,7},{5,4},{6,5},{7,6},{8,11},{9,8},{10,9... | collective-permute-start | bytes 786440 | tf_op jit(solution)/shard_map/ppermute | solution.py:28
where the time goes:
time: 52.6 us; the launch traced here: 52.5 us
  starting transfers between devices  21.4 us (41%)
  Pallas kernels  16 us (30%)
  waiting for transfers between devices  13.9 us (26%)
  local copies, waits for them, and re-layouts  1 us (2%)
    ppermute x6, starting transfers between devices, passed_round(): return lax.ppermute(x, ('energy', 'mom'), pairs)  16.9 us
    ppermute x6, waiting for transfers between devices, passed_round(): return lax.ppermute(x, ('energy', 'mom'), pairs)  13.9 us
    pallas_call x5, Pallas kernels, sums_call(): pl.pallas_call(kernel, out_shape=jax.ShapeDtypeStruct((count, parts, size...  7.22 us
    ppermute x2, starting transfers between devices, passed_along(): return lax.ppermute(x, axis, pairs)  4.48 us
    pallas_call x1, Pallas kernels, finish_call(): pl.pallas_call(kernel, grid=(len(energies),), out_shape=jax.ShapeDtypeStr...  2.72 us
    pallas_call x2, Pallas kernels, pair_call(): pl.pallas_call(kernel, out_shape=jax.ShapeDtypeStruct(pair.shape, pair.dt...  2.38 us
    pallas_call x1, Pallas kernels, early_call(): pl.pallas_call(kernel, out_shape=jax.ShapeDtypeStruct((count, parts, size...  2.15 us
    pallas_call x2, Pallas kernels, add_call(): pl.pallas_call(kernel, grid=(1,), out_shape=jax.ShapeDtypeStruct(out.shap...  1.5 us
  transfers between devices with their start and end apart: 8, of which 3 were waited for; matrix products, arithmetic and copies ran while one was open for 0% of the time, Pallas kernels for 29%

commit v1 on v0

--- a/solution.py
+++ b/solution.py
@@ -341,8 +341,8 @@
     own_top = own[last:]
     tops = {q: passed_round(own_top, q, q) for q in ups}
     made, high_1 = send(high, (1, True), own_top, early=True)
+    made, high_2 = send(high, (1, False), *made)
     below = passed_along(after(own_top, *made), "energy", 1)
-    made, high_2 = send(high, (1, False), *made)
     block = after(own, *made)
     own_high = sums_call(high, [(radius, own_slots(block))], args, own, jnp.float32)
     pair = sums_call((0, 1), [(radius, own_slots(block, below))], args, own, jnp.float32)

time: 52.6 us -> 52.5 us (level)
  starting transfers between devices: 21.4 us -> 25.5 us
  waiting for transfers between devices: 13.9 us -> 9.82 us
    ppermute x6, waiting for transfers between devices: 13.9 us -> 9.82 us  [passed_round(): return lax.ppermute(x, ('energy', 'mom'), pairs)]
    ppermute x6, starting transfers between devices: 16.9 us -> 20 us  [passed_round(): return lax.ppermute(x, ('energy', 'mom'), pairs)]
    ppermute x2, starting transfers between devices: 4.48 us -> 5.42 us  [passed_along(): return lax.ppermute(x, axis, pairs)]
where the time goes in v1:
time: 52.5 us; the launch traced here: 52.3 us
  starting transfers between devices  25.5 us (49%)
  Pallas kernels  15.9 us (30%)
  waiting for transfers between devices  9.82 us (19%)
  local copies, waits for them, and re-layouts  1 us (2%)
    ppermute x6, starting transfers between devices, passed_round(): return lax.ppermute(x, ('energy', 'mom'), pairs)  20 us
    ppermute x6, waiting for transfers between devices, passed_round(): return lax.ppermute(x, ('energy', 'mom'), pairs)  9.82 us
    pallas_call x5, Pallas kernels, sums_call(): pl.pallas_call(kernel, out_shape=jax.ShapeDtypeStruct((count, parts, size...  7.22 us
    ppermute x2, starting transfers between devices, passed_along(): return lax.ppermute(x, axis, pairs)  5.42 us
    pallas_call x1, Pallas kernels, finish_call(): pl.pallas_call(kernel, grid=(len(energies),), out_shape=jax.ShapeDtypeStr...  2.69 us
    pallas_call x2, Pallas kernels, pair_call(): pl.pallas_call(kernel, out_shape=jax.ShapeDtypeStruct(pair.shape, pair.dt...  2.38 us
    pallas_call x1, Pallas kernels, early_call(): pl.pallas_call(kernel, out_shape=jax.ShapeDtypeStruct((count, parts, size...  2.15 us
    pallas_call x2, Pallas kernels, add_call(): pl.pallas_call(kernel, grid=(1,), out_shape=jax.ShapeDtypeStruct(out.shap...  1.5 us
  transfers between devices with their start and end apart: 8, of which 3 were waited for; matrix products, arithmetic and copies ran while one was open for 0% of the time, Pallas kernels for 29%

profile of v1, /device:TPU:0, one launch (start us, length us, event | category | flops | bytes accessed | tf_op | source)
XLA Modules:
  0.0 52.3 jit_solution(12866613215684768839)
XLA Ops:
  0.0 1.0 %slice_bitcast_fusion = bf16[1,2,256,256]{3,2,1,0:T(8,128)(2,1)S(1)} fusion(bf16[1,1,4,2,256,256]{5,4,3,2,1,0:T(8,128)(2,1)} %param.4), kind=kLoop, calls=%fused_computation | loop fusion | bytes 524288 | tf_op jit(solution)/shard_map/slice | solution.py:341
  1.0 3.1 %collective-permute-start.1 = (bf16[1,2,256,256]{3,2,1,0:T(8,128)(2,1)S(1)}, bf16[1,2,256,256]{3,2,1,0:T(8,128)(2,1)S(1)}, u32[]{:S(2)}, u32[]{:S(2)}) collective-permute-start(bf16[1,2,256,256]{3,2,1,0:T(8,128)(2,1)S(1)} %slice_bitcast_fusion), channel_id=1, source_target_pairs={{0,1},{1,2},{2,3},{3,0},{4,5},{5,6},{6,7},{7,4},{8,9},{9,10},{10,1... | collective-permute-start | bytes 786440 | tf_op jit(solution)/shard_map/ppermute | solution.py:28
  4.1 2.1 %shard_map.46 = bf16[2,2,256,256]{3,2,1,0:T(8,128)(2,1)} custom-call(s32[2,3]{1,0:T(2,128)} %bitcast.12, bf16[2,256,256]{2,1,0:T(8,128)(2,1)} %refs_1_.1, bf16[3,1024,256]{2,1,0:T(8,128)(2,1)} %refs_2_.1, bf16[4,2,256,256]{3,2,1,0:T(8,128)(2,1)} %bitcast.5), custom_call_target="tpu_custom_call" | custom-call | flops 8589934592 | bytes 16777216 | tf_op jit(solution)/shard_map/pallas_call | solution.py:207
  6.2 1.6 %collective-permute-start.3 = (bf16[2,2,256,256]{3,2,1,0:T(8,128)(2,1)}, bf16[2,2,256,256]{3,2,1,0:T(8,128)(2,1)S(1)}, u32[]{:S(2)}, u32[]{:S(2)}) collective-permute-start(bf16[2,2,256,256]{3,2,1,0:T(8,128)(2,1)} %shard_map.46), channel_id=1, source_target_pairs={{0,1},{1,2},{2,3},{3,0},{4,7},{5,4},{6,5},{7,6},{8,9},{9,10},{10,1... | collective-permute-start | bytes 1572872 | tf_op jit(solution)/shard_map/ppermute | solution.py:28
  7.9 1.6 %shard_map.47 = bf16[2,2,256,256]{3,2,1,0:T(8,128)(2,1)S(1)} custom-call(s32[2,3]{1,0:T(2,128)S(1)} %bitcast.13, bf16[2,256,256]{2,1,0:T(8,128)(2,1)S(1)} %copy-done.2, bf16[3,1024,256]{2,1,0:T(8,128)(2,1)S(1)} %copy-done.1, bf16[4,2,256,256]{3,2,1,0:T(8,128)(2,1)S(1)} %bitcast.6), custom_call_target="tpu_custom_call" | custom-call | flops 8589934592 | bytes 16777216 | tf_op jit(solution)/shard_map/pallas_call | solution.py:167
  9.5 2.3 %collective-permute-start.4 = (bf16[2,2,256,256]{3,2,1,0:T(8,128)(2,1)S(1)}, bf16[2,2,256,256]{3,2,1,0:T(8,128)(2,1)S(1)}, u32[]{:S(2)}, u32[]{:S(2)}) collective-permute-start(bf16[2,2,256,256]{3,2,1,0:T(8,128)(2,1)S(1)} %shard_map.47), channel_id=1, source_target_pairs={{0,3},{1,0},{2,1},{3,2},{4,5},{5,6},{6,7},{7,4},{8,11},{9,8},{10,9... | collective-permute-start | bytes 1572872 | tf_op jit(solution)/shard_map/ppermute | solution.py:28
  11.8 1.3 %collective-permute-start = (bf16[1,2,256,256]{3,2,1,0:T(8,128)(2,1)S(1)}, bf16[1,2,256,256]{3,2,1,0:T(8,128)(2,1)S(1)}, u32[]{:S(2)}, u32[]{:S(2)}) collective-permute-start(bf16[1,2,256,256]{3,2,1,0:T(8,128)(2,1)S(1)} %slice_bitcast_fusion), channel_id=1, source_target_pairs={{0,4},{4,8},{8,12},{12,16},{16,20},{20,24},{24,28},{1,5},{5,9},{9,... | collective-permute-start | bytes 786440 | tf_op jit(solution)/shard_map/ppermute | solution.py:18
  13.1 1.6 %shard_map.53.refs_3_ = f32[2,2,256,256]{3,2,1,0:T(8,128)S(1)} custom-call(s32[2,3]{1,0:T(2,128)S(1)} %bitcast.14, bf16[2,256,256]{2,1,0:T(8,128)(2,1)S(1)} %copy-done.2, bf16[3,1024,256]{2,1,0:T(8,128)(2,1)S(1)} %copy-done.1, bf16[4,2,256,256]{3,2,1,0:T(8,128)(2,1)S(1)} %bitcast.7), custom_call_target="tpu_custom_call" | custom-call | flops 8589934592 | bytes 16777216 | tf_op jit(solution)/shard_map/pallas_call | solution.py:167
  14.7 0.0 collective-permute-done.1.refs_6_
  14.8 0.1 collective-permute-start.5
  14.8 4.1 %collective-permute-start.2 = (bf16[1,2,256,256]{3,2,1,0:T(8,128)(2,1)S(1)}, bf16[1,2,256,256]{3,2,1,0:T(8,128)(2,1)S(1)}, u32[]{:S(2)}, u32[]{:S(2)}) collective-permute-start(bf16[1,2,256,256]{3,2,1,0:T(8,128)(2,1)S(1)} %collective-permute-done.1.refs_6_), channel_id=1, source_target_pairs={{0,4},{4,8},{8,12},{12,16},{16,20},{20,24},{24,28},{1,5},{5,9},{9,... | collective-permute-start | bytes 786440 | tf_op jit(solution)/shard_map/ppermute | solution.py:18
  19.0 1.6 %shard_map.48.pair_ref = f32[2,2,256,256]{3,2,1,0:T(8,128)S(1)} custom-call(s32[2,3]{1,0:T(2,128)S(1)} %bitcast.15, bf16[2,256,256]{2,1,0:T(8,128)(2,1)S(1)} %copy-done.2, bf16[3,1024,256]{2,1,0:T(8,128)(2,1)S(1)} %copy-done.1, bf16[4,2,256,256]{3,2,1,0:T(8,128)(2,1)S(1)} %bitcast.9, bf16[1,2,256,256]{3,2,1,0:T(8,128)(2,1)S(1)} %collective-permute-done.refs_1_), custom_call_target="tpu_custom_call" | custom-call | flops 8589934592 | bytes 16777216 | tf_op jit(solution)/shard_map/pallas_call | solution.py:167
  20.6 3.5 %collective-permute-done.3.refs_1_.refs_4_ = bf16[2,2,256,256]{3,2,1,0:T(8,128)(2,1)S(1)} collective-permute-done((bf16[2,2,256,256]{3,2,1,0:T(8,128)(2,1)}, bf16[2,2,256,256]{3,2,1,0:T(8,128)(2,1)S(1)}, u32[]{:S(2)}, u32[]{:S(2)}) %collective-permute-start.3) | collective-permute-done | bytes 524320 | tf_op jit(solution)/shard_map/ppermute | solution.py:28
  24.1 1.2 %shard_map.51 = bf16[1,2,256,256]{3,2,1,0:T(8,128)(2,1)S(1)} custom-call(s32[2,3]{1,0:T(2,128)S(1)} %bitcast.16, bf16[2,256,256]{2,1,0:T(8,128)(2,1)S(1)} %copy-done.2, bf16[3,1024,256]{2,1,0:T(8,128)(2,1)S(1)} %copy-done.1, bf16[4,2,256,256]{3,2,1,0:T(8,128)(2,1)S(1)} %bitcast.10), custom_call_target="tpu_custom_call" | custom-call | flops 4294967296 | bytes 16777216 | tf_op jit(solution)/shard_map/pallas_call | solution.py:167
  25.3 12.5 %collective-permute-start.7 = (bf16[1,2,256,256]{3,2,1,0:T(8,128)(2,1)S(1)}, bf16[1,2,256,256]{3,2,1,0:T(8,128)(2,1)S(1)}, u32[]{:S(2)}, u32[]{:S(2)}) collective-permute-start(bf16[1,2,256,256]{3,2,1,0:T(8,128)(2,1)S(1)} %shard_map.51), channel_id=1, source_target_pairs={{0,3},{1,0},{2,1},{3,2},{4,7},{5,4},{6,5},{7,6},{8,11},{9,8},{10,9... | collective-permute-start | bytes 786440 | tf_op jit(solution)/shard_map/ppermute | solution.py:28
  37.8 1.2 %shard_map.52 = bf16[1,2,256,256]{3,2,1,0:T(8,128)(2,1)S(1)} custom-call(s32[2,3]{1,0:T(2,128)S(1)} %bitcast.17, bf16[2,256,256]{2,1,0:T(8,128)(2,1)S(1)} %copy-done.2, bf16[3,1024,256]{2,1,0:T(8,128)(2,1)S(1)} %copy-done.1, bf16[4,2,256,256]{3,2,1,0:T(8,128)(2,1)S(1)} %bitcast.11, bf16[1,2,256,256]{3,2,1,0:T(8,128)(2,1)S(1)} %collective-permute-done.refs_1_), custom_call_target="tpu_custom_call" | custom-call | flops 4294967296 | bytes 16777216 | tf_op jit(solution)/shard_map/pallas_call | solution.py:167
  39.0 0.5 collective-permute-start.6
  39.5 2.7 %shard_map.54.refs_1_ = bf16[4,2,256,256]{3,2,1,0:T(8,128)(2,1)} custom-call(s32[2,3]{1,0:T(2,128)S(1)} %bitcast.18, bf16[2,256,256]{2,1,0:T(8,128)(2,1)S(1)} %copy-done.2, bf16[3,1024,256]{2,1,0:T(8,128)(2,1)S(1)} %copy-done.1, f32[2,2,256,256]{3,2,1,0:T(8,128)S(1)} %shard_map.53.refs_3_, ...), custom_call_target="tpu_custom_call" | custom-call | flops 8589934592 | bytes 16777216 | tf_op jit(solution)/shard_map/pallas_call | solution.py:300
  42.2 1.2 %shard_map.49.pair_ref = f32[2,2,256,256]{3,2,1,0:T(8,128)S(1)} custom-call(s32[2,3]{1,0:T(2,128)S(1)} %bitcast.19, bf16[2,256,256]{2,1,0:T(8,128)(2,1)S(1)} %copy-done.2, bf16[3,1024,256]{2,1,0:T(8,128)(2,1)S(1)} %copy-done.1, f32[2,2,256,256]{3,2,1,0:T(8,128)S(1)} %shard_map.48.pair_ref, bf16[1,2,256,256]{3,2,1,0:T(8,128)(2,1)S(1)} %collective-permute-done.2.refs_0_, ...), custom_call_target="tpu_custom_call" | custom-call | flops 4294967296 | bytes 16777216 | tf_op jit(solution)/shard_map/pallas_call | solution.py:234
  43.4 1.2 %shard_map.50.pair_ref = f32[2,2,256,256]{3,2,1,0:T(8,128)S(1)} custom-call(s32[2,3]{1,0:T(2,128)S(1)} %bitcast.20, bf16[2,256,256]{2,1,0:T(8,128)(2,1)S(1)} %copy-done.2, bf16[3,1024,256]{2,1,0:T(8,128)(2,1)S(1)} %copy-done.1, f32[2,2,256,256]{3,2,1,0:T(8,128)S(1)} %shard_map.49.pair_ref, bf16[1,2,256,256]{3,2,1,0:T(8,128)(2,1)S(1)} %collective-permute-done.5.refs_0_), custom_call_target="tpu_custom_call" | custom-call | flops 4294967296 | bytes 16777216 | tf_op jit(solution)/shard_map/pallas_call | solution.py:234
  44.6 1.4 %collective-permute-done.7.refs_0_ = bf16[1,2,256,256]{3,2,1,0:T(8,128)(2,1)S(1)} collective-permute-done((bf16[1,2,256,256]{3,2,1,0:T(8,128)(2,1)S(1)}, bf16[1,2,256,256]{3,2,1,0:T(8,128)(2,1)S(1)}, u32[]{:S(2)}, u32[]{:S(2)}) %collective-permute-start.7) | collective-permute-done | bytes 262176 | tf_op jit(solution)/shard_map/ppermute | solution.py:28
  46.0 0.7 %shard_map.55.refs_1_ = bf16[4,2,256,256]{3,2,1,0:T(8,128)(2,1)} custom-call(f32[2,2,256,256]{3,2,1,0:T(8,128)S(1)} %shard_map.50.pair_ref, bf16[1,2,256,256]{3,2,1,0:T(8,128)(2,1)S(1)} %collective-permute-done.7.refs_0_, bf16[4,2,256,256]{3,2,1,0:T(8,128)(2,1)} %shard_map.54.refs_1_), custom_call_target="tpu_custom_call", output_to_operand_aliasing={{}: (2, {})} | custom-call | flops 8589934592 | bytes 16777216 | tf_op jit(solution)/shard_map/pallas_call | solution.py:254
  46.7 4.9 %collective-permute-done.6.refs_0_ = bf16[1,2,256,256]{3,2,1,0:T(8,128)(2,1)S(1)} collective-permute-done((bf16[1,2,256,256]{3,2,1,0:T(8,128)(2,1)S(1)}, bf16[1,2,256,256]{3,2,1,0:T(8,128)(2,1)S(1)}, u32[]{:S(2)}, u32[]{:S(2)}) %collective-permute-start.6) | collective-permute-done | bytes 262176 | tf_op jit(solution)/shard_map/ppermute | solution.py:28
  51.6 0.7 %shard_map.56 = bf16[4,2,256,256]{3,2,1,0:T(8,128)(2,1)} custom-call(f32[2,2,256,256]{3,2,1,0:T(8,128)S(1)} %shard_map.50.pair_ref, bf16[1,2,256,256]{3,2,1,0:T(8,128)(2,1)S(1)} %collective-permute-done.6.refs_0_, bf16[4,2,256,256]{3,2,1,0:T(8,128)(2,1)} %shard_map.55.refs_1_), custom_call_target="tpu_custom_call", output_to_operand_aliasing={{}: (2, {})} | custom-call | flops 8589934592 | bytes 16777216 | tf_op jit(solution)/shard_map/pallas_call | solution.py:254
  (13 shorter events, 0.0 us)
Async XLA Ops:
  1.0 13.8 %collective-permute-start.1 = (bf16[1,2,256,256]{3,2,1,0:T(8,128)(2,1)S(1)}, bf16[1,2,256,256]{3,2,1,0:T(8,128)(2,1)S(1)}, u32[]{:S(2)}, u32[]{:S(2)}) collective-permute-start(bf16[1,2,256,256]{3,2,1,0:T(8,128)(2,1)S(1)} %slice_bitcast_fusion), channel_id=1, source_target_pairs={{0,1},{1,2},{2,3},{3,0},{4,5},{5,6},{6,7},{7,4},{8,9},{9,10},{10,1... | collective-permute-start | bytes 786440 | tf_op jit(solution)/shard_map/ppermute | solution.py:28
  4.0 3.8 %copy-start = (bf16[1,1,4,2,256,256]{5,4,3,2,1,0:T(8,128)(2,1)S(1)}, bf16[1,1,4,2,256,256]{5,4,3,2,1,0:T(8,128)(2,1)}, u32[]{:S(2)}) copy-start(bf16[1,1,4,2,256,256]{5,4,3,2,1,0:T(8,128)(2,1)} %param.4) | copy-start | bytes 3145732
  4.0 3.8 %copy-start.1 = (bf16[3,1024,256]{2,1,0:T(8,128)(2,1)S(1)}, bf16[3,1024,256]{2,1,0:T(8,128)(2,1)}, u32[]{:S(2)}) copy-start(bf16[3,1024,256]{2,1,0:T(8,128)(2,1)} %refs_2_.1) | copy-start | bytes 4718596
  4.1 3.8 %copy-start.2 = (bf16[2,256,256]{2,1,0:T(8,128)(2,1)S(1)}, bf16[2,256,256]{2,1,0:T(8,128)(2,1)}, u32[]{:S(2)}) copy-start(bf16[2,256,256]{2,1,0:T(8,128)(2,1)} %refs_1_.1) | copy-start | bytes 786436
  4.1 3.8 %copy-start.3 = (s32[3,2]{0,1:T(2,128)S(1)}, s32[3,2]{0,1:T(2,128)}, u32[]{:S(2)}) copy-start(s32[3,2]{0,1:T(2,128)} %param.7) | copy-start | bytes 76
  6.2 17.9 %collective-permute-start.3 = (bf16[2,2,256,256]{3,2,1,0:T(8,128)(2,1)}, bf16[2,2,256,256]{3,2,1,0:T(8,128)(2,1)S(1)}, u32[]{:S(2)}, u32[]{:S(2)}) collective-permute-start(bf16[2,2,256,256]{3,2,1,0:T(8,128)(2,1)} %shard_map.46), channel_id=1, source_target_pairs={{0,1},{1,2},{2,3},{3,0},{4,7},{5,4},{6,5},{7,6},{8,9},{9,10},{10,1... | collective-permute-start | bytes 1572872 | tf_op jit(solution)/shard_map/ppermute | solution.py:28
  9.5 28.3 %collective-permute-start.4 = (bf16[2,2,256,256]{3,2,1,0:T(8,128)(2,1)S(1)}, bf16[2,2,256,256]{3,2,1,0:T(8,128)(2,1)S(1)}, u32[]{:S(2)}, u32[]{:S(2)}) collective-permute-start(bf16[2,2,256,256]{3,2,1,0:T(8,128)(2,1)S(1)} %shard_map.47), channel_id=1, source_target_pairs={{0,3},{1,0},{2,1},{3,2},{4,5},{5,6},{6,7},{7,4},{8,11},{9,8},{10,9... | collective-permute-start | bytes 1572872 | tf_op jit(solution)/shard_map/ppermute | solution.py:28
  11.8 7.2 %collective-permute-start = (bf16[1,2,256,256]{3,2,1,0:T(8,128)(2,1)S(1)}, bf16[1,2,256,256]{3,2,1,0:T(8,128)(2,1)S(1)}, u32[]{:S(2)}, u32[]{:S(2)}) collective-permute-start(bf16[1,2,256,256]{3,2,1,0:T(8,128)(2,1)S(1)} %slice_bitcast_fusion), channel_id=1, source_target_pairs={{0,4},{4,8},{8,12},{12,16},{16,20},{20,24},{24,28},{1,5},{5,9},{9,... | collective-permute-start | bytes 786440 | tf_op jit(solution)/shard_map/ppermute | solution.py:18
  14.8 28.6 %collective-permute-start.5 = (bf16[1,2,256,256]{3,2,1,0:T(8,128)(2,1)S(1)}, bf16[1,2,256,256]{3,2,1,0:T(8,128)(2,1)S(1)}, u32[]{:S(2)}, u32[]{:S(2)}) collective-permute-start(bf16[1,2,256,256]{3,2,1,0:T(8,128)(2,1)S(1)} %slice.11), channel_id=1, source_target_pairs={{0,1},{1,2},{2,3},{3,0},{4,5},{5,6},{6,7},{7,4},{8,9},{9,10},{10,1... | collective-permute-start | bytes 786440 | tf_op jit(solution)/shard_map/ppermute | solution.py:28
  14.8 27.3 %collective-permute-start.2 = (bf16[1,2,256,256]{3,2,1,0:T(8,128)(2,1)S(1)}, bf16[1,2,256,256]{3,2,1,0:T(8,128)(2,1)S(1)}, u32[]{:S(2)}, u32[]{:S(2)}) collective-permute-start(bf16[1,2,256,256]{3,2,1,0:T(8,128)(2,1)S(1)} %collective-permute-done.1.refs_6_), channel_id=1, source_target_pairs={{0,4},{4,8},{8,12},{12,16},{16,20},{20,24},{24,28},{1,5},{5,9},{9,... | collective-permute-start | bytes 786440 | tf_op jit(solution)/shard_map/ppermute | solution.py:18
  25.3 20.7 %collective-permute-start.7 = (bf16[1,2,256,256]{3,2,1,0:T(8,128)(2,1)S(1)}, bf16[1,2,256,256]{3,2,1,0:T(8,128)(2,1)S(1)}, u32[]{:S(2)}, u32[]{:S(2)}) collective-permute-start(bf16[1,2,256,256]{3,2,1,0:T(8,128)(2,1)S(1)} %shard_map.51), channel_id=1, source_target_pairs={{0,3},{1,0},{2,1},{3,2},{4,7},{5,4},{6,5},{7,6},{8,11},{9,8},{10,9... | collective-permute-start | bytes 786440 | tf_op jit(solution)/shard_map/ppermute | solution.py:28
  39.0 12.6 %collective-permute-start.6 = (bf16[1,2,256,256]{3,2,1,0:T(8,128)(2,1)S(1)}, bf16[1,2,256,256]{3,2,1,0:T(8,128)(2,1)S(1)}, u32[]{:S(2)}, u32[]{:S(2)}) collective-permute-start(bf16[1,2,256,256]{3,2,1,0:T(8,128)(2,1)S(1)} %shard_map.52), channel_id=1, source_target_pairs={{0,3},{1,0},{2,1},{3,2},{4,7},{5,4},{6,5},{7,6},{8,11},{9,8},{10,9... | collective-permute-start | bytes 786440 | tf_op jit(solution)/shard_map/ppermute | solution.py:28
